TPU v7x, 128 devices: a whole 4x4x4 slice. The times are simulated.
128 devices in a mesh: ctx: 32 (over x_lo, z, y), tp: 4 (over x_hi, core).
Axes of the slice: x: 4 (x_hi: 2, x_lo: 2; x = x_hi * 2 + x_lo), y: 4, z: 4, core: 2. Of those that a mesh axis runs over, the one named last changes fastest.
Arguments:
- stream_one: bfloat16 [12288, 8192], P('ctx', 'tp'), may hold values from -6 to 6
- stream_two: bfloat16 [12288, 8192], P('ctx', 'tp'), may hold values from -6 to 6
- stream_value: bfloat16 [12288, 8192], P('ctx', 'tp'), may hold values from -6 to 6
- short_stream_taps: bfloat16 [3, 7, 8192], P(None, None, 'tp'), may hold values from -6 to 6
- medium_filter: bfloat16 [512, 128], P('tp'), may hold values from -1.25 to 1.25
- residual: bfloat16 [12288, 8192], P('ctx', 'tp'), may hold values from -60 to 60
- norm_gain: bfloat16 [8192], P('tp'), may hold values from 0.5 to 1.5
- queries: bfloat16 [12288, 4096], P('ctx', 'tp'), may hold values from -12 to 12
- keys: bfloat16 [12288, 512], P('ctx', 'tp'), may hold values from -6 to 6
- values: bfloat16 [12288, 512], P('ctx', 'tp'), may hold values from -6 to 6
Outputs:
- normed: bfloat16 [12288, 8192], P('ctx', 'tp')
- attended: bfloat16 [12288, 4096], P('ctx', 'tp')
All inputs are finite; a program needn't handle non-finite values.
Results may differ from a plain program's by a relative error of at most 0.0065.
Values may be sent and summed in bfloat16 or wider, within the bound.
No kernel may reach another device: no remote copies, remote signals or barrier semaphores. Data moves between devices by JAX's collectives and lax.ppermute only.
A program may use at most 128 MiB of HBM per device.

v0:
```python
import math

import jax
import jax.numpy as jnp
from jax import lax
from jax.sharding import PartitionSpec as P

D = 8192
GROUP = 16
SHORT = 7
MEDIUM_TAPS = 128
QH = 32
KVH = 4
HD = 128


def passed_along(value, axis, steps):
    count = lax.axis_size(axis)
    leading, last = (max(0, -steps), min(count, count - steps))
    return lax.ppermute(value, axis, [(source, source + steps) for source in range(leading, last)])


def causal_sum(extended, taps, count):
    total = jnp.zeros((count, extended.shape[1]), jnp.float32)
    for j in range(SHORT):
        total = total + taps[j].astype(jnp.float32)[None, :] * extended[
            SHORT - 1 - j : SHORT - 1 - j + count
        ].astype(jnp.float32)
    return total


def medium_conv(context_window, filters, rows):
    groups = filters.shape[0]
    block = MEDIUM_TAPS // 2
    span = block + MEDIUM_TAPS - 1
    filter_tap_index = (
        jnp.arange(block, dtype=jnp.int32)[:, None]
        + (MEDIUM_TAPS - 1)
        - jnp.arange(span, dtype=jnp.int32)[None, :]
    )
    selector = (
        jnp.arange(MEDIUM_TAPS, dtype=jnp.int32)[:, None, None] == filter_tap_index[None]
    ).astype(jnp.bfloat16)
    selector = selector.reshape(MEDIUM_TAPS, block * span)
    toeplitz = jnp.dot(filters, selector, preferred_element_type=jnp.float32).astype(jnp.bfloat16)
    toeplitz = toeplitz.reshape(groups, block, span)
    count = rows // block
    windows = jnp.stack(
        [context_window[number * block : number * block + span] for number in range(count)], axis=0
    )
    windows = windows.reshape(count, span, groups, GROUP)
    result = jnp.einsum("gts,bsgc->btgc", toeplitz, windows, preferred_element_type=jnp.float32)
    return result.reshape(rows, groups * GROUP)


def fresh_state(query_group_rows):
    count, heads, ratio, size = query_group_rows.shape
    top = jnp.full((heads, ratio, count), -1e30, jnp.float32)
    totals = jnp.zeros((heads, ratio, count), jnp.float32)
    accum = jnp.zeros((heads, ratio, count, size), jnp.float32)
    return (top, totals, accum)


def advance(state, query_group_rows, first, key_tile_block, value_block, key_start):
    count = query_group_rows.shape[0]
    last = first + count - 1
    scale = 1.0 / math.sqrt(HD)

    def update(carried):
        top, totals, accum = carried
        scores = (
            jnp.einsum(
                "ompx,zmx->mpoz",
                query_group_rows,
                key_tile_block,
                preferred_element_type=jnp.float32,
            )
            * scale
        )
        query_pos = first + jnp.arange(count, dtype=jnp.int32)
        key_pos = key_start + jnp.arange(key_tile_block.shape[0], dtype=jnp.int32)
        allowed = (key_pos[None, :] <= query_pos[:, None])[None, None]
        scores = jnp.where(allowed, scores, -1e30)
        new_top = jnp.maximum(top, jnp.max(scores, axis=-1))
        factor = jnp.exp(top - new_top)
        probs = jnp.where(allowed, jnp.exp(scores - new_top[..., None]), 0.0)
        totals = totals * factor + jnp.sum(probs, axis=-1)
        accum = accum * factor[..., None] + jnp.einsum(
            "ubaq,quy->ubay",
            probs.astype(jnp.bfloat16),
            value_block,
            preferred_element_type=jnp.float32,
        )
        return (new_top, totals, accum)

    def unchanged(carried):
        return carried

    return lax.cond(key_start <= last, update, unchanged, state)


def finish(state):
    top, totals, accum = state
    heads, ratio, count, size = accum.shape
    result = (accum / totals[..., None]).astype(jnp.bfloat16)
    return result.transpose(2, 0, 1, 3).reshape(count, heads * ratio * size)


def attend_groups(groups, keys, values):
    block = keys.shape[0]
    heads = keys.shape[1] // HD
    initial = tuple((fresh_state(group[0]) for group in groups))
    key_piece = lax.all_gather(keys, "ctx", axis=0, tiled=True)
    value_piece = lax.all_gather(values, "ctx", axis=0, tiled=True)

    def step(number, carried):
        key_start = number * block
        key_tile_block = lax.dynamic_slice_in_dim(key_piece, number * block, block, 0).reshape(
            block, heads, HD
        )
        value_block = lax.dynamic_slice_in_dim(value_piece, number * block, block, 0).reshape(
            block, heads, HD
        )
        return tuple(
            (
                advance(
                    carried[item],
                    groups[item][0],
                    groups[item][1],
                    key_tile_block,
                    value_block,
                    key_start,
                )
                for item in range(len(groups))
            )
        )

    final = lax.fori_loop(0, key_piece.shape[0] // block, step, initial)
    return tuple((finish(state) for state in final))


def shards(
    stream_one,
    stream_two,
    stream_value,
    short_stream_taps,
    medium_filter,
    residual,
    norm_gain,
    queries,
    keys,
    values,
):
    rows, width = stream_one.shape
    stacked = jnp.concatenate([stream_one, stream_two, stream_value], axis=1)
    taps = short_stream_taps.transpose(1, 0, 2).reshape(SHORT, 3 * width)
    rim = passed_along(stacked[rows - (SHORT - 1) :], "ctx", 1)
    shorts = causal_sum(jnp.concatenate([rim, stacked], axis=0), taps, rows)
    mixed_in = (shorts[:, :width] * shorts[:, 2 * width :]).astype(jnp.bfloat16)
    earlier = passed_along(mixed_in[rows - (MEDIUM_TAPS - 1) :], "ctx", 1)
    context_window = jnp.concatenate([earlier, mixed_in], axis=0)
    gate_short = shorts[:, width : 2 * width]
    medium = medium_conv(context_window, medium_filter, rows)
    branch_sum = residual.astype(jnp.float32) + gate_short * medium
    squares = lax.psum(jnp.sum(branch_sum * branch_sum, axis=1), "tp")
    scaling = lax.rsqrt(squares / D + 1e-06)
    normed = (branch_sum * scaling[:, None] * norm_gain.astype(jnp.float32)[None, :]).astype(
        jnp.bfloat16
    )
    heads = keys.shape[1] // HD
    ratio = QH // KVH
    shaped = queries.reshape(rows, heads, ratio, HD)
    position = lax.axis_index("ctx")
    outputs = attend_groups(((shaped, position * rows),), keys, values)
    attended = outputs[0]
    return (normed, attended)


def solution(mesh):
    in_specs = (
        P("ctx", "tp"),
        P("ctx", "tp"),
        P("ctx", "tp"),
        P(None, None, "tp"),
        P("tp", None),
        P("ctx", "tp"),
        P("tp"),
        P("ctx", "tp"),
        P("ctx", "tp"),
        P("ctx", "tp"),
    )
    out_specs = (P("ctx", "tp"), P("ctx", "tp"))
    return jax.shard_map(shards, mesh=mesh, in_specs=in_specs, out_specs=out_specs, check_vma=False)
```

profile of v0, /device:TPU:122, one launch (start us, length us, event | category | flops | bytes accessed | tf_op | source)
XLA Modules:
  0.0 524.7 jit_solution(5170785362521459285)
XLA Ops:
  21.9 5.9 %collective-permute-done = bf16[6,6144]{1,0:T(8,128)(2,1)} collective-permute-done((bf16[6,6144]{1,0:T(8,128)(2,1)S(1)}, bf16[6,6144]{1,0:T(8,128)(2,1)}, u32[]{:S(2)}, u32[]{:S(2)}) %collective-permute-start) | collective-permute-done | bytes 73760 | tf_op jit(solution)/shard_map/ppermute | solution.py:20
  30.1 17.7 %maximum_maximum_fusion = bf16[390,6144]{0,1:T(8,128)(2,1)} fusion(bf16[384,2048]{0,1:T(8,128)(2,1)} %copy.36, bf16[384,2048]{0,1:T(8,128)(2,1)S(1)} %copy.35, bf16[384,2048]{0,1:T(8,128)(2,1)S(1)} %copy.34, bf16[6,6144]{0,1:T(8,128)(2,1)} %copy.38), kind=kLoop, calls=%fused_computation.30 | loop fusion | flops 19169280 | bytes 9584640 | tf_op jit(solution)/shard_map/concatenate | solution.py:158
  47.8 26.9 %multiply_add_fusion = f32[384,6144]{0,1:T(8,128)S(1)} fusion(bf16[390,6144]{0,1:T(8,128)(2,1)} %maximum_maximum_fusion, f32[6144]{0:T(1024)S(1)} %bitcast.96, f32[6144]{0:T(1024)S(1)} %bitcast.97, f32[6144]{0:T(1024)S(1)} %bitcast.98, f32[6144]{0:T(1024)S(1)} %bitcast.99, f32[6144]{0:T(1024)S(1)} %bitcast.100, f32[6144]{0:T(1024)S(1)} %bitcast.101, ...), kind=kLoop, calls=%fused_computation.29 | loop fusion | flops 58982400 | bytes 42639360 | tf_op jit(solution)/shard_map/add | solution.py:26
  74.8 3.6 copy-done.2
  84.5 4.5 reshape.230
  89.1 6.8 %copy.46 = bf16[128,64,191,1]{2,1,3,0:T(8,128)(2,1)} copy(bf16[128,64,191,1]{0,2,1,3:T(8,128)(2,1)} %bitcast.81) | data formatting | bytes 6258688 | tf_op jit(solution)/shard_map/reshape | solution.py:46
  99.2 3.5 pad_maximum_fusion.1
  109.7 5.8 %convolution_bitcast_fusion = f32[6,64,128,16]{1,3,0,2:T(8,128)S(1)} fusion(bf16[6,191,128,16]{1,3,0,2:T(8,128)(2,1)} %constant_dynamic-update-slice_fusion, bf16[128,64,191,1]{2,1,3,0:T(8,128)(2,1)} %copy.46), kind=kOutput, calls=%fused_computation.41 | convolution fusion | flops 300417024 | bytes 10969088 | tf_op jit(solution)/shard_map/gts,bsgc->btgc/dot_general | solution.py:52
  115.5 6.4 %copy.40 = f32[6,64,128,16]{1,0,3,2:T(8,128)} copy(f32[6,64,128,16]{1,3,0,2:T(8,128)S(1)} %convolution_bitcast_fusion) | data formatting | bytes 6291456 | tf_op jit(solution)/shard_map/gts,bsgc->btgc/transpose | solution.py:52
  121.9 7.2 %reshape.231 = f32[384,2048]{0,1:T(8,128)} reshape(f32[6,64,128,16]{1,0,3,2:T(8,128)} %copy.40) | data formatting | bytes 6291456 | tf_op jit(solution)/shard_map/reshape | solution.py:53
  129.1 3.4 multiply_reduce_fusion
  132.6 8.4 %psum.7 = f32[384]{0:T(512)S(1)} all-reduce(f32[384]{0:T(512)S(1)} %multiply_reduce_fusion), channel_id=1, replica_groups=mesh['ctx'=32,'tp'=4] {'tp'}, use_global_device_ids=true, to_apply=%region_1.0 | all-reduce | flops 384 | bytes 3072 | tf_op jit(solution)/shard_map/psum | solution.py:165
  141.0 4.6 multiply_convert_fusion
  148.2 17.5 %all-gather.3.cloned.1.call-done = bf16[12288,128]{1,0:T(8,128)(2,1)} async-done(((bf16[384,128]{1,0:T(8,128)(2,1)}), bf16[12288,128]{1,0:T(8,128)(2,1)}) %all-gather.3.cloned.1.call-update) | async-done | bytes 3145744 | tf_op jit(solution)/shard_map/all_gather | solution.py:113
  165.6 157.6 %all-gather.5.cloned.1.call-done = bf16[12288,128]{1,0:T(8,128)(2,1)} async-done(((bf16[384,128]{1,0:T(8,128)(2,1)}), bf16[12288,128]{1,0:T(8,128)(2,1)}) %all-gather.5.cloned.1.call-update) | async-done | bytes 3145744 | tf_op jit(solution)/shard_map/all_gather | solution.py:114
  323.4 192.4 %while.19 = (s32[]{:T(128)}, f32[1,8,384]{2,1,0:T(8,128)S(1)}, f32[1,8,384]{2,1,0:T(8,128)S(1)}, f32[1,8,384,128]{3,2,1,0:T(8,128)S(1)}, s32[]{:T(128)}, /*index...) while((s32[]{:T(128)}, f32[1,8,384]{2,1,0:T(8,128)S(1)}, ...), condition=%wide.region_7.8_spmd, body=%wide.region_2.7_spmd.sunk | while | flops 620259072 | bytes 19077424 | solution.py:138
  323.4 6.0 %conditional.2 = ((f32[1,8,384]{2,1,0:T(8,128)S(1)}, f32[1,8,384]{2,1,0:T(8,128)S(1)}, f32[1,8,384,128]{3,2,1,0:T(8,128)S(1)})) conditional(s32[]{:T(128)} %convert_element_type.197, (f32[1,8,384]{2,1,0:T(8,128)S(1)}, f32[1,8,384]{2,1,0:T(8,128)S(1)}, f32[1,8,384,128]{3,2,1,0:T(8,128)S(1)}) %tuple.76, (s32[]{:T(128)}, s32[]{:T(128)}, ...), branch_computations={%region_3.0_spmd, %region_4.6_spmd} | conditional | flops 620259072 | bytes 19077202 | solution.py:99
  329.4 6.0 %conditional.2 = ((f32[1,8,384]{2,1,0:T(8,128)S(1)}, f32[1,8,384]{2,1,0:T(8,128)S(1)}, f32[1,8,384,128]{3,2,1,0:T(8,128)S(1)})) conditional(s32[]{:T(128)} %convert_element_type.197, (f32[1,8,384]{2,1,0:T(8,128)S(1)}, f32[1,8,384]{2,1,0:T(8,128)S(1)}, f32[1,8,384,128]{3,2,1,0:T(8,128)S(1)}) %tuple.76, (s32[]{:T(128)}, s32[]{:T(128)}, ...), branch_computations={%region_3.0_spmd, %region_4.6_spmd} | conditional | flops 620259072 | bytes 19077202 | solution.py:99
  335.4 6.0 %conditional.2 = ((f32[1,8,384]{2,1,0:T(8,128)S(1)}, f32[1,8,384]{2,1,0:T(8,128)S(1)}, f32[1,8,384,128]{3,2,1,0:T(8,128)S(1)})) conditional(s32[]{:T(128)} %convert_element_type.197, (f32[1,8,384]{2,1,0:T(8,128)S(1)}, f32[1,8,384]{2,1,0:T(8,128)S(1)}, f32[1,8,384,128]{3,2,1,0:T(8,128)S(1)}) %tuple.76, (s32[]{:T(128)}, s32[]{:T(128)}, ...), branch_computations={%region_3.0_spmd, %region_4.6_spmd} | conditional | flops 620259072 | bytes 19077202 | solution.py:99
  341.4 6.0 %conditional.2 = ((f32[1,8,384]{2,1,0:T(8,128)S(1)}, f32[1,8,384]{2,1,0:T(8,128)S(1)}, f32[1,8,384,128]{3,2,1,0:T(8,128)S(1)})) conditional(s32[]{:T(128)} %convert_element_type.197, (f32[1,8,384]{2,1,0:T(8,128)S(1)}, f32[1,8,384]{2,1,0:T(8,128)S(1)}, f32[1,8,384,128]{3,2,1,0:T(8,128)S(1)}) %tuple.76, (s32[]{:T(128)}, s32[]{:T(128)}, ...), branch_computations={%region_3.0_spmd, %region_4.6_spmd} | conditional | flops 620259072 | bytes 19077202 | solution.py:99
  343.4 2.8 bitcast_add_fusion
  347.5 6.0 %conditional.2 = ((f32[1,8,384]{2,1,0:T(8,128)S(1)}, f32[1,8,384]{2,1,0:T(8,128)S(1)}, f32[1,8,384,128]{3,2,1,0:T(8,128)S(1)})) conditional(s32[]{:T(128)} %convert_element_type.197, (f32[1,8,384]{2,1,0:T(8,128)S(1)}, f32[1,8,384]{2,1,0:T(8,128)S(1)}, f32[1,8,384,128]{3,2,1,0:T(8,128)S(1)}) %tuple.76, (s32[]{:T(128)}, s32[]{:T(128)}, ...), branch_computations={%region_3.0_spmd, %region_4.6_spmd} | conditional | flops 620259072 | bytes 19077202 | solution.py:99
  349.4 2.8 bitcast_add_fusion
  353.5 6.0 %conditional.2 = ((f32[1,8,384]{2,1,0:T(8,128)S(1)}, f32[1,8,384]{2,1,0:T(8,128)S(1)}, f32[1,8,384,128]{3,2,1,0:T(8,128)S(1)})) conditional(s32[]{:T(128)} %convert_element_type.197, (f32[1,8,384]{2,1,0:T(8,128)S(1)}, f32[1,8,384]{2,1,0:T(8,128)S(1)}, f32[1,8,384,128]{3,2,1,0:T(8,128)S(1)}) %tuple.76, (s32[]{:T(128)}, s32[]{:T(128)}, ...), branch_computations={%region_3.0_spmd, %region_4.6_spmd} | conditional | flops 620259072 | bytes 19077202 | solution.py:99
  355.5 2.8 bitcast_add_fusion
  359.5 6.0 %conditional.2 = ((f32[1,8,384]{2,1,0:T(8,128)S(1)}, f32[1,8,384]{2,1,0:T(8,128)S(1)}, f32[1,8,384,128]{3,2,1,0:T(8,128)S(1)})) conditional(s32[]{:T(128)} %convert_element_type.197, (f32[1,8,384]{2,1,0:T(8,128)S(1)}, f32[1,8,384]{2,1,0:T(8,128)S(1)}, f32[1,8,384,128]{3,2,1,0:T(8,128)S(1)}) %tuple.76, (s32[]{:T(128)}, s32[]{:T(128)}, ...), branch_computations={%region_3.0_spmd, %region_4.6_spmd} | conditional | flops 620259072 | bytes 19077202 | solution.py:99
  361.5 2.8 bitcast_add_fusion
  365.5 6.0 %conditional.2 = ((f32[1,8,384]{2,1,0:T(8,128)S(1)}, f32[1,8,384]{2,1,0:T(8,128)S(1)}, f32[1,8,384,128]{3,2,1,0:T(8,128)S(1)})) conditional(s32[]{:T(128)} %convert_element_type.197, (f32[1,8,384]{2,1,0:T(8,128)S(1)}, f32[1,8,384]{2,1,0:T(8,128)S(1)}, f32[1,8,384,128]{3,2,1,0:T(8,128)S(1)}) %tuple.76, (s32[]{:T(128)}, s32[]{:T(128)}, ...), branch_computations={%region_3.0_spmd, %region_4.6_spmd} | conditional | flops 620259072 | bytes 19077202 | solution.py:99
  367.5 2.8 bitcast_add_fusion
  371.5 6.0 %conditional.2 = ((f32[1,8,384]{2,1,0:T(8,128)S(1)}, f32[1,8,384]{2,1,0:T(8,128)S(1)}, f32[1,8,384,128]{3,2,1,0:T(8,128)S(1)})) conditional(s32[]{:T(128)} %convert_element_type.197, (f32[1,8,384]{2,1,0:T(8,128)S(1)}, f32[1,8,384]{2,1,0:T(8,128)S(1)}, f32[1,8,384,128]{3,2,1,0:T(8,128)S(1)}) %tuple.76, (s32[]{:T(128)}, s32[]{:T(128)}, ...), branch_computations={%region_3.0_spmd, %region_4.6_spmd} | conditional | flops 620259072 | bytes 19077202 | solution.py:99
  373.5 2.8 bitcast_add_fusion
  377.5 6.0 %conditional.2 = ((f32[1,8,384]{2,1,0:T(8,128)S(1)}, f32[1,8,384]{2,1,0:T(8,128)S(1)}, f32[1,8,384,128]{3,2,1,0:T(8,128)S(1)})) conditional(s32[]{:T(128)} %convert_element_type.197, (f32[1,8,384]{2,1,0:T(8,128)S(1)}, f32[1,8,384]{2,1,0:T(8,128)S(1)}, f32[1,8,384,128]{3,2,1,0:T(8,128)S(1)}) %tuple.76, (s32[]{:T(128)}, s32[]{:T(128)}, ...), branch_computations={%region_3.0_spmd, %region_4.6_spmd} | conditional | flops 620259072 | bytes 19077202 | solution.py:99
  379.5 2.8 bitcast_add_fusion
  383.5 6.0 %conditional.2 = ((f32[1,8,384]{2,1,0:T(8,128)S(1)}, f32[1,8,384]{2,1,0:T(8,128)S(1)}, f32[1,8,384,128]{3,2,1,0:T(8,128)S(1)})) conditional(s32[]{:T(128)} %convert_element_type.197, (f32[1,8,384]{2,1,0:T(8,128)S(1)}, f32[1,8,384]{2,1,0:T(8,128)S(1)}, f32[1,8,384,128]{3,2,1,0:T(8,128)S(1)}) %tuple.76, (s32[]{:T(128)}, s32[]{:T(128)}, ...), branch_computations={%region_3.0_spmd, %region_4.6_spmd} | conditional | flops 620259072 | bytes 19077202 | solution.py:99
  385.5 2.8 bitcast_add_fusion
  389.5 6.0 %conditional.2 = ((f32[1,8,384]{2,1,0:T(8,128)S(1)}, f32[1,8,384]{2,1,0:T(8,128)S(1)}, f32[1,8,384,128]{3,2,1,0:T(8,128)S(1)})) conditional(s32[]{:T(128)} %convert_element_type.197, (f32[1,8,384]{2,1,0:T(8,128)S(1)}, f32[1,8,384]{2,1,0:T(8,128)S(1)}, f32[1,8,384,128]{3,2,1,0:T(8,128)S(1)}) %tuple.76, (s32[]{:T(128)}, s32[]{:T(128)}, ...), branch_computations={%region_3.0_spmd, %region_4.6_spmd} | conditional | flops 620259072 | bytes 19077202 | solution.py:99
  391.5 2.8 bitcast_add_fusion
  395.6 6.0 %conditional.2 = ((f32[1,8,384]{2,1,0:T(8,128)S(1)}, f32[1,8,384]{2,1,0:T(8,128)S(1)}, f32[1,8,384,128]{3,2,1,0:T(8,128)S(1)})) conditional(s32[]{:T(128)} %convert_element_type.197, (f32[1,8,384]{2,1,0:T(8,128)S(1)}, f32[1,8,384]{2,1,0:T(8,128)S(1)}, f32[1,8,384,128]{3,2,1,0:T(8,128)S(1)}) %tuple.76, (s32[]{:T(128)}, s32[]{:T(128)}, ...), branch_computations={%region_3.0_spmd, %region_4.6_spmd} | conditional | flops 620259072 | bytes 19077202 | solution.py:99
  397.5 2.8 bitcast_add_fusion
  401.6 6.0 %conditional.2 = ((f32[1,8,384]{2,1,0:T(8,128)S(1)}, f32[1,8,384]{2,1,0:T(8,128)S(1)}, f32[1,8,384,128]{3,2,1,0:T(8,128)S(1)})) conditional(s32[]{:T(128)} %convert_element_type.197, (f32[1,8,384]{2,1,0:T(8,128)S(1)}, f32[1,8,384]{2,1,0:T(8,128)S(1)}, f32[1,8,384,128]{3,2,1,0:T(8,128)S(1)}) %tuple.76, (s32[]{:T(128)}, s32[]{:T(128)}, ...), branch_computations={%region_3.0_spmd, %region_4.6_spmd} | conditional | flops 620259072 | bytes 19077202 | solution.py:99
  403.6 2.8 bitcast_add_fusion
  407.6 6.0 %conditional.2 = ((f32[1,8,384]{2,1,0:T(8,128)S(1)}, f32[1,8,384]{2,1,0:T(8,128)S(1)}, f32[1,8,384,128]{3,2,1,0:T(8,128)S(1)})) conditional(s32[]{:T(128)} %convert_element_type.197, (f32[1,8,384]{2,1,0:T(8,128)S(1)}, f32[1,8,384]{2,1,0:T(8,128)S(1)}, f32[1,8,384,128]{3,2,1,0:T(8,128)S(1)}) %tuple.76, (s32[]{:T(128)}, s32[]{:T(128)}, ...), branch_computations={%region_3.0_spmd, %region_4.6_spmd} | conditional | flops 620259072 | bytes 19077202 | solution.py:99
  409.6 2.8 bitcast_add_fusion
  413.6 6.0 %conditional.2 = ((f32[1,8,384]{2,1,0:T(8,128)S(1)}, f32[1,8,384]{2,1,0:T(8,128)S(1)}, f32[1,8,384,128]{3,2,1,0:T(8,128)S(1)})) conditional(s32[]{:T(128)} %convert_element_type.197, (f32[1,8,384]{2,1,0:T(8,128)S(1)}, f32[1,8,384]{2,1,0:T(8,128)S(1)}, f32[1,8,384,128]{3,2,1,0:T(8,128)S(1)}) %tuple.76, (s32[]{:T(128)}, s32[]{:T(128)}, ...), branch_computations={%region_3.0_spmd, %region_4.6_spmd} | conditional | flops 620259072 | bytes 19077202 | solution.py:99
  419.6 6.0 %conditional.2 = ((f32[1,8,384]{2,1,0:T(8,128)S(1)}, f32[1,8,384]{2,1,0:T(8,128)S(1)}, f32[1,8,384,128]{3,2,1,0:T(8,128)S(1)})) conditional(s32[]{:T(128)} %convert_element_type.197, (f32[1,8,384]{2,1,0:T(8,128)S(1)}, f32[1,8,384]{2,1,0:T(8,128)S(1)}, f32[1,8,384,128]{3,2,1,0:T(8,128)S(1)}) %tuple.76, (s32[]{:T(128)}, s32[]{:T(128)}, ...), branch_computations={%region_3.0_spmd, %region_4.6_spmd} | conditional | flops 620259072 | bytes 19077202 | solution.py:99
  421.6 2.8 bitcast_add_fusion
  425.6 6.0 %conditional.2 = ((f32[1,8,384]{2,1,0:T(8,128)S(1)}, f32[1,8,384]{2,1,0:T(8,128)S(1)}, f32[1,8,384,128]{3,2,1,0:T(8,128)S(1)})) conditional(s32[]{:T(128)} %convert_element_type.197, (f32[1,8,384]{2,1,0:T(8,128)S(1)}, f32[1,8,384]{2,1,0:T(8,128)S(1)}, f32[1,8,384,128]{3,2,1,0:T(8,128)S(1)}) %tuple.76, (s32[]{:T(128)}, s32[]{:T(128)}, ...), branch_computations={%region_3.0_spmd, %region_4.6_spmd} | conditional | flops 620259072 | bytes 19077202 | solution.py:99
  431.6 6.0 %conditional.2 = ((f32[1,8,384]{2,1,0:T(8,128)S(1)}, f32[1,8,384]{2,1,0:T(8,128)S(1)}, f32[1,8,384,128]{3,2,1,0:T(8,128)S(1)})) conditional(s32[]{:T(128)} %convert_element_type.197, (f32[1,8,384]{2,1,0:T(8,128)S(1)}, f32[1,8,384]{2,1,0:T(8,128)S(1)}, f32[1,8,384,128]{3,2,1,0:T(8,128)S(1)}) %tuple.76, (s32[]{:T(128)}, s32[]{:T(128)}, ...), branch_computations={%region_3.0_spmd, %region_4.6_spmd} | conditional | flops 620259072 | bytes 19077202 | solution.py:99
  437.6 6.0 %conditional.2 = ((f32[1,8,384]{2,1,0:T(8,128)S(1)}, f32[1,8,384]{2,1,0:T(8,128)S(1)}, f32[1,8,384,128]{3,2,1,0:T(8,128)S(1)})) conditional(s32[]{:T(128)} %convert_element_type.197, (f32[1,8,384]{2,1,0:T(8,128)S(1)}, f32[1,8,384]{2,1,0:T(8,128)S(1)}, f32[1,8,384,128]{3,2,1,0:T(8,128)S(1)}) %tuple.76, (s32[]{:T(128)}, s32[]{:T(128)}, ...), branch_computations={%region_3.0_spmd, %region_4.6_spmd} | conditional | flops 620259072 | bytes 19077202 | solution.py:99
  443.7 6.0 %conditional.2 = ((f32[1,8,384]{2,1,0:T(8,128)S(1)}, f32[1,8,384]{2,1,0:T(8,128)S(1)}, f32[1,8,384,128]{3,2,1,0:T(8,128)S(1)})) conditional(s32[]{:T(128)} %convert_element_type.197, (f32[1,8,384]{2,1,0:T(8,128)S(1)}, f32[1,8,384]{2,1,0:T(8,128)S(1)}, f32[1,8,384,128]{3,2,1,0:T(8,128)S(1)}) %tuple.76, (s32[]{:T(128)}, s32[]{:T(128)}, ...), branch_computations={%region_3.0_spmd, %region_4.6_spmd} | conditional | flops 620259072 | bytes 19077202 | solution.py:99
  449.7 6.0 %conditional.2 = ((f32[1,8,384]{2,1,0:T(8,128)S(1)}, f32[1,8,384]{2,1,0:T(8,128)S(1)}, f32[1,8,384,128]{3,2,1,0:T(8,128)S(1)})) conditional(s32[]{:T(128)} %convert_element_type.197, (f32[1,8,384]{2,1,0:T(8,128)S(1)}, f32[1,8,384]{2,1,0:T(8,128)S(1)}, f32[1,8,384,128]{3,2,1,0:T(8,128)S(1)}) %tuple.76, (s32[]{:T(128)}, s32[]{:T(128)}, ...), branch_computations={%region_3.0_spmd, %region_4.6_spmd} | conditional | flops 620259072 | bytes 19077202 | solution.py:99
  455.7 6.0 %conditional.2 = ((f32[1,8,384]{2,1,0:T(8,128)S(1)}, f32[1,8,384]{2,1,0:T(8,128)S(1)}, f32[1,8,384,128]{3,2,1,0:T(8,128)S(1)})) conditional(s32[]{:T(128)} %convert_element_type.197, (f32[1,8,384]{2,1,0:T(8,128)S(1)}, f32[1,8,384]{2,1,0:T(8,128)S(1)}, f32[1,8,384,128]{3,2,1,0:T(8,128)S(1)}) %tuple.76, (s32[]{:T(128)}, s32[]{:T(128)}, ...), branch_computations={%region_3.0_spmd, %region_4.6_spmd} | conditional | flops 620259072 | bytes 19077202 | solution.py:99
  461.7 6.0 %conditional.2 = ((f32[1,8,384]{2,1,0:T(8,128)S(1)}, f32[1,8,384]{2,1,0:T(8,128)S(1)}, f32[1,8,384,128]{3,2,1,0:T(8,128)S(1)})) conditional(s32[]{:T(128)} %convert_element_type.197, (f32[1,8,384]{2,1,0:T(8,128)S(1)}, f32[1,8,384]{2,1,0:T(8,128)S(1)}, f32[1,8,384,128]{3,2,1,0:T(8,128)S(1)}) %tuple.76, (s32[]{:T(128)}, s32[]{:T(128)}, ...), branch_computations={%region_3.0_spmd, %region_4.6_spmd} | conditional | flops 620259072 | bytes 19077202 | solution.py:99
  463.7 2.8 bitcast_add_fusion
  467.7 6.0 %conditional.2 = ((f32[1,8,384]{2,1,0:T(8,128)S(1)}, f32[1,8,384]{2,1,0:T(8,128)S(1)}, f32[1,8,384,128]{3,2,1,0:T(8,128)S(1)})) conditional(s32[]{:T(128)} %convert_element_type.197, (f32[1,8,384]{2,1,0:T(8,128)S(1)}, f32[1,8,384]{2,1,0:T(8,128)S(1)}, f32[1,8,384,128]{3,2,1,0:T(8,128)S(1)}) %tuple.76, (s32[]{:T(128)}, s32[]{:T(128)}, ...), branch_computations={%region_3.0_spmd, %region_4.6_spmd} | conditional | flops 620259072 | bytes 19077202 | solution.py:99
  473.7 6.0 %conditional.2 = ((f32[1,8,384]{2,1,0:T(8,128)S(1)}, f32[1,8,384]{2,1,0:T(8,128)S(1)}, f32[1,8,384,128]{3,2,1,0:T(8,128)S(1)})) conditional(s32[]{:T(128)} %convert_element_type.197, (f32[1,8,384]{2,1,0:T(8,128)S(1)}, f32[1,8,384]{2,1,0:T(8,128)S(1)}, f32[1,8,384,128]{3,2,1,0:T(8,128)S(1)}) %tuple.76, (s32[]{:T(128)}, s32[]{:T(128)}, ...), branch_computations={%region_3.0_spmd, %region_4.6_spmd} | conditional | flops 620259072 | bytes 19077202 | solution.py:99
  479.7 6.0 %conditional.2 = ((f32[1,8,384]{2,1,0:T(8,128)S(1)}, f32[1,8,384]{2,1,0:T(8,128)S(1)}, f32[1,8,384,128]{3,2,1,0:T(8,128)S(1)})) conditional(s32[]{:T(128)} %convert_element_type.197, (f32[1,8,384]{2,1,0:T(8,128)S(1)}, f32[1,8,384]{2,1,0:T(8,128)S(1)}, f32[1,8,384,128]{3,2,1,0:T(8,128)S(1)}) %tuple.76, (s32[]{:T(128)}, s32[]{:T(128)}, ...), branch_computations={%region_3.0_spmd, %region_4.6_spmd} | conditional | flops 620259072 | bytes 19077202 | solution.py:99
  485.7 6.0 %conditional.2 = ((f32[1,8,384]{2,1,0:T(8,128)S(1)}, f32[1,8,384]{2,1,0:T(8,128)S(1)}, f32[1,8,384,128]{3,2,1,0:T(8,128)S(1)})) conditional(s32[]{:T(128)} %convert_element_type.197, (f32[1,8,384]{2,1,0:T(8,128)S(1)}, f32[1,8,384]{2,1,0:T(8,128)S(1)}, f32[1,8,384,128]{3,2,1,0:T(8,128)S(1)}) %tuple.76, (s32[]{:T(128)}, s32[]{:T(128)}, ...), branch_computations={%region_3.0_spmd, %region_4.6_spmd} | conditional | flops 620259072 | bytes 19077202 | solution.py:99
  491.8 6.0 %conditional.2 = ((f32[1,8,384]{2,1,0:T(8,128)S(1)}, f32[1,8,384]{2,1,0:T(8,128)S(1)}, f32[1,8,384,128]{3,2,1,0:T(8,128)S(1)})) conditional(s32[]{:T(128)} %convert_element_type.197, (f32[1,8,384]{2,1,0:T(8,128)S(1)}, f32[1,8,384]{2,1,0:T(8,128)S(1)}, f32[1,8,384,128]{3,2,1,0:T(8,128)S(1)}) %tuple.76, (s32[]{:T(128)}, s32[]{:T(128)}, ...), branch_computations={%region_3.0_spmd, %region_4.6_spmd} | conditional | flops 620259072 | bytes 19077202 | solution.py:99
  493.7 2.8 bitcast_add_fusion
  497.8 6.0 %conditional.2 = ((f32[1,8,384]{2,1,0:T(8,128)S(1)}, f32[1,8,384]{2,1,0:T(8,128)S(1)}, f32[1,8,384,128]{3,2,1,0:T(8,128)S(1)})) conditional(s32[]{:T(128)} %convert_element_type.197, (f32[1,8,384]{2,1,0:T(8,128)S(1)}, f32[1,8,384]{2,1,0:T(8,128)S(1)}, f32[1,8,384,128]{3,2,1,0:T(8,128)S(1)}) %tuple.76, (s32[]{:T(128)}, s32[]{:T(128)}, ...), branch_computations={%region_3.0_spmd, %region_4.6_spmd} | conditional | flops 620259072 | bytes 19077202 | solution.py:99
  503.8 6.0 %conditional.2 = ((f32[1,8,384]{2,1,0:T(8,128)S(1)}, f32[1,8,384]{2,1,0:T(8,128)S(1)}, f32[1,8,384,128]{3,2,1,0:T(8,128)S(1)})) conditional(s32[]{:T(128)} %convert_element_type.197, (f32[1,8,384]{2,1,0:T(8,128)S(1)}, f32[1,8,384]{2,1,0:T(8,128)S(1)}, f32[1,8,384,128]{3,2,1,0:T(8,128)S(1)}) %tuple.76, (s32[]{:T(128)}, s32[]{:T(128)}, ...), branch_computations={%region_3.0_spmd, %region_4.6_spmd} | conditional | flops 620259072 | bytes 19077202 | solution.py:99
  505.8 2.8 bitcast_add_fusion
  509.8 6.0 %conditional.2 = ((f32[1,8,384]{2,1,0:T(8,128)S(1)}, f32[1,8,384]{2,1,0:T(8,128)S(1)}, f32[1,8,384,128]{3,2,1,0:T(8,128)S(1)})) conditional(s32[]{:T(128)} %convert_element_type.197, (f32[1,8,384]{2,1,0:T(8,128)S(1)}, f32[1,8,384]{2,1,0:T(8,128)S(1)}, f32[1,8,384,128]{3,2,1,0:T(8,128)S(1)}) %tuple.76, (s32[]{:T(128)}, s32[]{:T(128)}, ...), branch_computations={%region_3.0_spmd, %region_4.6_spmd} | conditional | flops 620259072 | bytes 19077202 | solution.py:99
  (295 shorter events, 182.2 us)
Async XLA Ops:
  7.2 74.7 %copy-start = (bf16[128,128]{1,0:T(8,128)(2,1)S(1)}, bf16[128,128]{1,0:T(8,128)(2,1)}, u32[]{:S(2)}) copy-start(bf16[128,128]{1,0:T(8,128)(2,1)} %param.18) | copy-start | bytes 98308
  7.2 158.5 %all-gather.3.cloned.1.call-start = ((), (), s32[]{:S(2)}) async-start(), calls=%async_computation | async-start | bytes 3244032 | tf_op jit(solution)/shard_map/all_gather | solution.py:113
  7.9 315.3 %all-gather.5.cloned.1.call-start = ((), (), s32[]{:S(2)}) async-start(), calls=%async_computation.1 | async-start | bytes 3244032 | tf_op jit(solution)/shard_map/all_gather | solution.py:114
  17.0 4.8 copy-start.5
  20.4 7.3 %collective-permute-start = (bf16[6,6144]{1,0:T(8,128)(2,1)S(1)}, bf16[6,6144]{1,0:T(8,128)(2,1)}, u32[]{:S(2)}, u32[]{:S(2)}) collective-permute-start(bf16[6,6144]{1,0:T(8,128)(2,1)S(1)} %copy.37), channel_id=1, source_target_pairs={{0,4},{4,8},{8,12},{12,16},{16,20},{20,24},{24,28},{28,32},{32,36}... | collective-permute-start | bytes 221192 | tf_op jit(solution)/shard_map/ppermute | solution.py:20
  74.7 3.6 copy-start.2
  79.7 19.5 %collective-permute-start.1 = (bf16[127,2048]{0,1:T(8,128)(2,1)}, bf16[127,2048]{0,1:T(8,128)(2,1)}, u32[]{:S(2)}, u32[]{:S(2)}) collective-permute-start(bf16[127,2048]{0,1:T(8,128)(2,1)} %slice.120), channel_id=1, source_target_pairs={{0,4},{4,8},{8,12},{12,16},{16,20},{20,24},{24,28},{28,32},{32,36}... | collective-permute-start | bytes 1560584 | tf_op jit(solution)/shard_map/ppermute | solution.py:20
  89.0 9.4 %copy-start.6 = (bf16[2048]{0:T(1024)(128)(2,1)S(1)}, bf16[2048]{0:T(1024)(128)(2,1)}, u32[]{:S(2)}) copy-start(bf16[2048]{0:T(1024)(128)(2,1)} %param.20) | copy-start | bytes 12292
  89.1 9.4 %copy-start.4 = (bf16[384,1024]{1,0:T(8,128)(2,1)S(1)}, bf16[384,1024]{1,0:T(8,128)(2,1)}, u32[]{:S(2)}) copy-start(bf16[384,1024]{1,0:T(8,128)(2,1)} %param.21) | copy-start | bytes 2359300
  121.9 7.2 %copy-start.3 = (bf16[384,2048]{0,1:T(8,128)(2,1)S(1)}, bf16[384,2048]{0,1:T(8,128)(2,1)}, u32[]{:S(2)}) copy-start(bf16[384,2048]{0,1:T(8,128)(2,1)} %copy.33) | copy-start | bytes 4718596
  515.8 2.1 copy-start.1
Sparse Core Ops, SparseCore 0:
  9.7 155.9 all-gather.2
  167.3 155.9 all-gather.4
where the time goes:
time: 527 us; the launch traced here: 525 us
  waiting for transfers between devices  182 us (35%)
  matrix products  155 us (29%)
  other arithmetic  102 us (19%)
  local copies, waits for them, and re-layouts  57 us (11%)
  between operations  14.3 us (3%)
  blocking collectives  8.41 us (2%)
    all_gather x1, waiting for transfers between devices, attend_groups(): value_piece = lax.all_gather(values, 'ctx', axis=0, tiled=True)  158 us
    dot_general x32, matrix products, update(): jnp.einsum('ubaq,quy->ubay', probs.astype(jnp.bfloat16), value_block, pre...  89.7 us
    dot_general x32, matrix products, update(): jnp.einsum('ompx,zmx->mpoz', query_group_rows, key_tile_block, preferred_...  56.9 us
    reduce_sum x32, other arithmetic, update(): totals = totals * factor + jnp.sum(probs, axis=-1)  36.8 us
    add x1, other arithmetic, causal_sum(): total + taps[j].astype(jnp.float32)[None, :] * extended[SHORT - 1 - j:SHO...  26.9 us
    unnamed x26, local copies, waits for them, and re-layouts  22.3 us
    concatenate x1, other arithmetic, shards(): shorts = causal_sum(jnp.concatenate([rim, stacked], axis=0), taps, rows)  17.7 us
    all_gather x1, waiting for transfers between devices, attend_groups(): key_piece = lax.all_gather(keys, 'ctx', axis=0, tiled=True)  17.5 us
  transfers between devices with their start and end apart: 4, of which 3 were waited for; matrix products, arithmetic and copies ran while one was open for 23% of the time, Pallas kernels for 0%

commit v1 on v0

v1 whole, which is shorter than its diff:
```python
import functools
import math

import jax
import jax.numpy as jnp
import numpy as np
from jax import lax
from jax.experimental import pallas as pl
from jax.experimental.pallas import tpu as pltpu
from jax.sharding import PartitionSpec as P

f32=jnp.float32; bf=jnp.bfloat16
SHORT=7; GROUP=16; LANES=128; EDGE=16; TAPS=128; BLK=64

def tail_kernel(one, two, val, taps, out, x_scr):
    keep = TAPS
    last = one.shape[0]
    t = taps[...].astype(f32)
    def short(ref, which, slot):
        x_scr[slot] = ref[last - keep - EDGE:, :].astype(f32)
        total = t[which, 0:1] * x_scr[slot, EDGE:EDGE + keep, :]
        for j in range(1, SHORT):
            total += t[which, j:j + 1] * x_scr[slot, EDGE - j:EDGE - j + keep, :]
        return total
    out[0:keep] = (short(one, 0, 0) * short(val, 2, 1)).astype(bf)
    for n, ref in enumerate((one, two, val)):
        out[keep + EDGE * n:keep + EDGE * (n + 1)] = ref[last - EDGE:, :]

def tail_call(one, two, val, taps):
    rows, width = one.shape
    spec = pl.BlockSpec((rows, LANES), lambda i: (0, i))
    out_rows = TAPS + 3 * EDGE
    return pl.pallas_call(tail_kernel, grid=(width // LANES,),
        in_specs=[spec] * 3 + [pl.BlockSpec((3, SHORT, LANES), lambda i: (0, 0, i))],
        out_specs=pl.BlockSpec((out_rows, LANES), lambda i: (0, i)),
        out_shape=jax.ShapeDtypeStruct((out_rows, width), bf),
        scratch_shapes=[pltpu.VMEM((2, TAPS + EDGE, LANES), f32)],
        name="mixed_tail")(one, two, val, taps)

def mixer_kernel(one, two, val, halo, taps, rev, res, branch, squares, x_scr, m_scr, t_scr):
    rows = one.shape[0]
    t = taps[...].astype(f32)
    def short(ref, n):
        lo = TAPS + EDGE * n
        x_scr[n, 0:EDGE] = halo[lo:lo + EDGE, :].astype(f32)
        x_scr[n, EDGE:] = ref[...].astype(f32)
        total = t[n, 0:1] * x_scr[n, EDGE:, :]
        for j in range(1, SHORT):
            total += t[n, j:j + 1] * x_scr[n, EDGE - j:EDGE - j + rows, :]
        return total
    m_scr[0:TAPS] = halo[0:TAPS]
    m_scr[TAPS:] = (short(one, 0) * short(val, 2)).astype(bf)
    gate = short(two, 1)
    groups = LANES // GROUP
    for g in range(groups):
        row = jnp.broadcast_to(rev[g:g + 1, :], (BLK, 2 * TAPS))
        rolled = pltpu.roll(row, 0, 1, stride=1, stride_axis=0)
        t_scr[g * BLK:(g + 1) * BLK] = rolled.astype(bf)
    lane = lax.broadcasted_iota(jnp.int32, (BLK, LANES), 1) // GROUP
    span = BLK + TAPS
    total = jnp.zeros((8, 128), f32)
    for pair in range(rows // (2 * BLK)):
        at = 2 * BLK * pair
        window = jnp.concatenate([m_scr[at:at + span], m_scr[at + BLK:at + BLK + span]], axis=1)
        wide = jnp.dot(t_scr[:, :span], window, preferred_element_type=f32)
        for half in range(2):
            r = slice(at + BLK * half, at + BLK * (half + 1))
            c = slice(LANES * half, LANES * (half + 1))
            medium = wide[0:BLK, c]
            for g in range(1, groups):
                medium = jnp.where(lane == g, wide[g * BLK:(g + 1) * BLK, c], medium)
            summed = res[r].astype(f32) + gate[r] * medium
            branch[r] = summed
            sq = summed * summed
            @pl.when(pl.program_id(0) == 0)
            def _(): squares[r] = sq
            @pl.when(pl.program_id(0) > 0)
            def _(): squares[r] += sq

def mixer_call(one, two, val, halo, taps, rev, res):
    rows, width = one.shape
    spec = pl.BlockSpec((rows, LANES), lambda i: (0, i))
    groups = LANES // GROUP
    return pl.pallas_call(mixer_kernel, grid=(width // LANES,),
        in_specs=[spec] * 3 + [pl.BlockSpec((halo.shape[0], LANES), lambda i: (0, i)),
            pl.BlockSpec((3, SHORT, LANES), lambda i: (0, 0, i)),
            pl.BlockSpec((groups, 2 * TAPS), lambda i: (i, 0)), spec],
        out_specs=[spec, pl.BlockSpec((rows, LANES), lambda i: (0, 0))],
        out_shape=[jax.ShapeDtypeStruct((rows, width), f32), jax.ShapeDtypeStruct((rows, LANES), f32)],
        scratch_shapes=[pltpu.VMEM((3, EDGE + rows, LANES), f32), pltpu.VMEM((TAPS + rows, LANES), bf),
            pltpu.VMEM((groups * BLK, 2 * TAPS), bf)],
        compiler_params=pltpu.CompilerParams(vmem_limit_bytes=32 * 2**20),
        name="mixer")(one, two, val, halo, taps, rev, res)

def reversed_taps(filters):
    flipped = filters.astype(f32)[:, ::-1]
    return jnp.pad(flipped, ((0, 0), (1, TAPS - 1)))


HD = 128
PAIR = 2
ONES = 16
EMPTY, FULL, DIAGONAL = 0, 1, 2
SCALE = math.log2(math.e) / math.sqrt(HD)


def pack_kernel(keys, values, packed):
    packed[:, :HD] = keys[...]
    turned = values[...].astype(f32).T.astype(bf)
    for part in range(values.shape[0] // HD):
        packed[part * HD:(part + 1) * HD, HD:] = turned[:, part * HD:(part + 1) * HD]


def pack_call(keys, values):
    return pl.pallas_call(pack_kernel, out_shape=jax.ShapeDtypeStruct((keys.shape[0], 2 * HD), bf),
                          name="pack_keys")(keys, values)


def turn_kernel(queries, turned):
    rows = queries.shape[0]
    for head in range(PAIR):
        wide = queries[:, head * HD:(head + 1) * HD].astype(f32).T * SCALE
        high = wide.astype(bf)
        columns = slice(head * rows, (head + 1) * rows)
        turned[0, :HD, columns] = high
        turned[0, HD:, columns] = (wide - high.astype(f32)).astype(bf)


def turn_call(queries):
    rows, width = queries.shape
    pairs = width // (PAIR * HD)
    return pl.pallas_call(turn_kernel, grid=(pairs,),
        in_specs=[pl.BlockSpec((rows, PAIR * HD), lambda i: (0, i))],
        out_specs=pl.BlockSpec((1, 2 * HD, PAIR * rows), lambda i: (i, 0, 0)),
        out_shape=jax.ShapeDtypeStruct((pairs, 2 * HD, PAIR * rows), bf),
        name="turn_queries")(queries)


def attend_kernel(first, last, sizes, pairs, rows, *refs):
    refs = list(refs)
    table, q_hbm = refs[0], refs[1]
    at = 2
    pieces = refs[at:at + len(sizes)]
    at += len(sizes)
    if not first:
        acc_in, top_in = refs[at:at + 2]
        at += 2
    if last:
        out = refs[at]
        at += 1
    else:
        acc_out, top_out = refs[at:at + 2]
        at += 2
    q, kv, acc, top, scores, probs, factors, load_sem, kv_sem, store_sem = refs[at:]
    shards = sum(sizes)
    me = lax.axis_index("ctx")
    count = table[me, 0]

    def kv_copies():
        number = 0
        for piece, size in zip(pieces, sizes):
            for index in range(size):
                slot = table[me, 1 + number]
                yield slot, pltpu.make_async_copy(piece.at[index], kv.at[jnp.maximum(slot, 0)], kv_sem.at[number])
                number += 1

    for slot, copy in kv_copies():
        pl.when(slot >= 0)(copy.start)
    loads = [pltpu.make_async_copy(q_hbm, q, load_sem.at[0])]
    if not first:
        loads.append(pltpu.make_async_copy(acc_in, acc, load_sem.at[1]))
        loads.append(pltpu.make_async_copy(top_in, top, load_sem.at[2]))
    for copy in loads:
        copy.start()
    blocks = kv.shape[0] // 2

    if first:
        acc[...] = jnp.zeros_like(acc)
        top[...] = jnp.full_like(top, -1e30)
    if shards % 2 or True:
        for block in range(blocks):
            @pl.when(table[me, 1 + shards] == block)
            def _():
                kv[2 * block + 1] = jnp.zeros(kv.shape[1:], kv.dtype)
    for slot, copy in kv_copies():
        pl.when(slot >= 0)(copy.wait)
    for copy in loads:
        copy.wait()

    def entry(number):
        code = table[me, 2 + shards + jnp.minimum(number, count - 1)]
        return code % 8, (code // 8) % 16, (code // 128) % 2, (code // 256) % 4, (code // 1024) % 4

    def multiply_keys(number, slot):
        pair, block = entry(number)[:2]
        k = jnp.concatenate([kv[2 * block, :, :HD], kv[2 * block + 1, :, :HD]], axis=0)
        k = jnp.concatenate([k, k], axis=1)
        scores[slot] = jnp.dot(k, q[pair], preferred_element_type=f32)

    def multiply_values(number, slot):
        pair, block = entry(number)[:2]
        parts = rows // HD
        v = jnp.concatenate([kv[2 * block + n // parts, (n % parts) * HD:(n % parts + 1) * HD, HD:]
                             for n in range(2 * parts)], axis=1)
        v = jnp.concatenate([v, jnp.ones((ONES, 2 * rows), bf)], axis=0)
        product = jnp.dot(v, probs[slot], preferred_element_type=f32)
        acc[pair] = acc[pair] * factors[slot, 0:1] + product

    def mask(number, slot):
        _, _, masked, mode0, mode1 = entry(number)

        @pl.when(masked == 1)
        def _():
            key = lax.broadcasted_iota(jnp.int32, (rows, rows), 0)
            query = lax.broadcasted_iota(jnp.int32, (rows, rows), 1)
            for half, mode in enumerate((mode0, mode1)):
                limit = jnp.where(mode == FULL, rows, jnp.where(mode == DIAGONAL, 0, -2 * rows))
                allowed = key - query <= limit
                for head in range(PAIR):
                    r = slice(half * rows, (half + 1) * rows)
                    c = slice(head * rows, (head + 1) * rows)
                    scores[slot, r, c] = jnp.where(allowed, scores[slot, r, c], -1e30)

    def half_step(number, slot):
        mask(number, slot)
        multiply_keys(number + 1, 1 - slot)
        multiply_values(jnp.maximum(number - 1, 0), 1 - slot)
        pair = entry(number)[0]
        s = scores[slot]
        old = top[pair, 0:1]
        new = jnp.maximum(old, jnp.max(s, axis=0, keepdims=True))
        factors[slot, 0:1] = jnp.exp2(old - new)
        top[pair, 0:1] = new
        probs[slot] = jnp.exp2(s - new).astype(bf)

    @pl.when(count > 0)
    def _():
        probs[1] = jnp.zeros(probs.shape[1:], bf)
        factors[1] = jnp.ones(factors.shape[1:], f32)
        multiply_keys(0, 0)

        @pl.loop(0, (count + 1) // 2)
        def _(step):
            half_step(2 * step, 0)
            @pl.when(2 * step + 1 < count)
            def _():
                half_step(2 * step + 1, 1)

        for parity in range(2):
            @pl.when((count - 1) % 2 == parity)
            def _():
                multiply_values(count - 1, parity)

    if last:
        for pair in range(pairs):
            for head in range(PAIR):
                c = slice(head * rows, (head + 1) * rows)
                value = acc[pair, :HD, c] / acc[pair, HD:HD + 1, c]
                at = (pair * PAIR + head) * HD
                out[:, at:at + HD] = value.T.astype(bf)
    else:
        stores = [pltpu.make_async_copy(acc, acc_out, store_sem.at[0]), pltpu.make_async_copy(top, top_out, store_sem.at[1])]
        for copy in stores:
            copy.start()
        for copy in stores:
            copy.wait()


def attend_call(table, turned, pieces, state, last, entries):
    pairs, _, wide = turned.shape
    rows = wide // PAIR
    sizes = tuple(piece.shape[0] for piece in pieces)
    shards = sum(sizes)
    slots = shards + shards % 2
    first = state is None
    acc_shape = jax.ShapeDtypeStruct((pairs, HD + ONES, wide), f32)
    top_shape = jax.ShapeDtypeStruct((pairs, 8, wide), f32)
    hbm = pl.BlockSpec(memory_space=pl.ANY)
    operands = [table, turned, *pieces] + ([] if first else list(state))
    if last:
        out_shape = jax.ShapeDtypeStruct((rows, pairs * PAIR * HD), bf)
        out_specs = pl.BlockSpec(memory_space=pltpu.VMEM)
    else:
        out_shape = [acc_shape, top_shape]
        out_specs = [hbm, hbm]
    return pl.pallas_call(
        functools.partial(attend_kernel, first, last, sizes, pairs, rows),
        in_specs=[pl.BlockSpec(memory_space=pltpu.SMEM)] + [hbm] * (len(operands) - 1),
        out_specs=out_specs,
        out_shape=out_shape,
        scratch_shapes=[
            pltpu.VMEM(turned.shape, bf),
            pltpu.VMEM((slots, rows, 2 * HD), bf),
            pltpu.VMEM(acc_shape.shape, f32),
            pltpu.VMEM(top_shape.shape, f32),
            pltpu.VMEM((2, 2 * rows, wide), f32),
            pltpu.VMEM((2, 2 * rows, wide), bf),
            pltpu.VMEM((2, 8, wide), f32),
            pltpu.SemaphoreType.DMA((3,)),
            pltpu.SemaphoreType.DMA((shards,)),
            pltpu.SemaphoreType.DMA((2,)),
        ],
        compiler_params=pltpu.CompilerParams(vmem_limit_bytes=48 * 2**20),
        cost_estimate=pl.CostEstimate(flops=entries * 8 * rows * rows * 4 * HD, bytes_accessed=4 * 2**20, transcendentals=0),
        name="attend",
    )(*operands)


def make_table(sources_of, pairs, offset=0):
    rows_out = []
    for me, sources in enumerate(sources_of):
        shards = len(sources)
        allowed = [n for n, source in enumerate(sources) if source <= me]
        slot = {n: at for at, n in enumerate(allowed)}
        modes = [DIAGONAL if sources[n] == me else FULL for n in allowed]
        odd = len(modes) % 2
        modes = modes + [EMPTY] * odd
        codes = []
        for block in range(len(modes) // 2):
            pair_modes = modes[2 * block:2 * block + 2]
            masked = int(pair_modes != [FULL, FULL])
            for pair in range(pairs):
                codes.append(pair + 8 * block + 128 * masked + 256 * pair_modes[0] + 1024 * pair_modes[1])
        most = pairs * ((shards + 1) // 2)
        line = [len(codes)] + [slot.get(n, -1) for n in range(shards)] + [len(modes) // 2 - 1 if odd else -1]
        rows_out.append(line + codes + [0] * (most - len(codes)))
    return np.array(rows_out, np.int32)


D = 8192
Z = Y = 4
PLANE = Z * Y


def split(i):
    return i // PLANE, (i // Y) % Z, i % Y


def neighbour(i, x=0, z=0, y=0):
    at_x, at_z, at_y = split(i)
    return (at_x + x) % 2 * PLANE + (at_z + z) % Z * Y + (at_y + y) % Y


def moved(value, x=0, z=0, y=0):
    pairs = [(i, neighbour(i, x, z, y)) for i in range(2 * PLANE)]
    return lax.ppermute(value, "ctx", pairs)


def gathered(first, axis, other):
    near = [first] + [moved(first, **{axis: step}) for step in (1, -1, 2)]
    line = jnp.stack(near)
    behind = moved(line, **{other: 1})
    ahead = moved(line, **{other: -1})
    half = line.shape[0] // 2
    low = moved(behind[:half], **{other: 1})
    high = moved(ahead[half:], **{other: -1})
    return near[1:], [behind, ahead], [low, high]


def sources_of(me, plane, axis, other):
    base = plane * PLANE + me % PLANE
    line = [neighbour(base, **{axis: -step}) for step in (0, 1, -1, 2)]
    def shifted(blocks, step):
        return [neighbour(b, **{other: -step}) for b in blocks]
    return line[1:], shifted(line, 1) + shifted(line, -1), shifted(line[:2], 2) + shifted(line[2:], -2)


def tables(pairs):
    everyone = range(2 * PLANE)
    chunks = [[[me, neighbour(me, x=1)] for me in everyone]]
    for stage in range(3):
        chunks.append([sources_of(me, 0, "z", "y")[stage] + sources_of(me, 1, "y", "z")[stage] for me in everyone])
    for me in everyone:
        assert sorted(sum((c[me] for c in chunks), [])) == list(everyone)
    return [make_table(c, pairs) for c in chunks]


def shards(stream_one, stream_two, stream_value, short_stream_taps, medium_filter, residual, norm_gain, queries, keys, values):
    rows, width = stream_one.shape
    pairs = queries.shape[1] // (PAIR * HD)
    own = pack_call(keys, values)
    other = moved(own, x=1)
    tail = tail_call(stream_one, stream_two, stream_value, short_stream_taps)
    halo = lax.ppermute(tail, "ctx", [(i, i + 1) for i in range(2 * PLANE - 1)])
    turned = turn_call(queries)
    low = lax.axis_index("ctx") < PLANE
    first = jnp.where(low, own, other)
    second = jnp.where(low, other, own)
    a = gathered(first, "z", "y")
    b = gathered(second, "y", "z")
    lists = tables(pairs)
    state = attend_call(lists[0], turned, [own[None], other[None]], None, False, pairs)
    state = attend_call(lists[1], turned, [p[None] for p in a[0] + b[0]], state, False, 3 * pairs)
    branch, squares = mixer_call(stream_one, stream_two, stream_value, halo, short_stream_taps, reversed_taps(medium_filter), residual)
    state = attend_call(lists[2], turned, a[1] + b[1], state, False, 8 * pairs)
    attended = attend_call(lists[3], turned, a[2] + b[2], state, True, 4 * pairs)
    total = lax.psum(jnp.sum(squares, axis=1), "tp")
    scaling = lax.rsqrt(total / D + 1e-06)
    normed = (branch * scaling[:, None] * norm_gain.astype(f32)[None, :]).astype(bf)
    return normed, attended


def solution(mesh):
    in_specs = (P("ctx", "tp"), P("ctx", "tp"), P("ctx", "tp"), P(None, None, "tp"), P("tp", None),
                P("ctx", "tp"), P("tp"), P("ctx", "tp"), P("ctx", "tp"), P("ctx", "tp"))
    return jax.shard_map(shards, mesh=mesh, in_specs=in_specs, out_specs=(P("ctx", "tp"), P("ctx", "tp")), check_vma=False)
```

time: 527 us -> 176 us (0.33)
  the two profiles are of different devices: /device:TPU:122 before, /device:TPU:102 now
where the time goes in v1:
time: 176 us; the launch traced here: 175 us
  Pallas kernels  123 us (70%)
  starting transfers between devices  26.3 us (15%)
  blocking collectives  7.17 us (4%)
  local copies, waits for them, and re-layouts  6.57 us (4%)
  waiting for transfers between devices  6.06 us (3%)
  other arithmetic  4.55 us (3%)
    pallas_call x4, Pallas kernels, attend_call(): pl.pallas_call(functools.partial(attend_kernel, first, last, sizes, pairs...  86.2 us
    ppermute x15, starting transfers between devices, moved(): return lax.ppermute(value, 'ctx', pairs)  23.7 us
    pallas_call x1, Pallas kernels, mixer_call(): pl.pallas_call(mixer_kernel, grid=(width // LANES,), in_specs=[spec] * 3...  21.4 us
    pallas_call x1, Pallas kernels, tail_call(): pl.pallas_call(tail_kernel, grid=(width // LANES,), in_specs=[spec] * 3 +...  10.4 us
    psum x1, blocking collectives, shards(): total = lax.psum(jnp.sum(squares, axis=1), 'tp')  7.17 us
    ppermute x15, waiting for transfers between devices, moved(): return lax.ppermute(value, 'ctx', pairs)  6.06 us
    pallas_call x1, Pallas kernels, turn_call(): pl.pallas_call(turn_kernel, grid=(pairs,), in_specs=[pl.BlockSpec((rows,...  3.66 us
  transfers between devices with their start and end apart: 16, of which 1 were waited for; matrix products, arithmetic and copies ran while one was open for 5% of the time, Pallas kernels for 56%

profile of v1, /device:TPU:102, one launch (start us, length us, event | category | flops | bytes accessed | tf_op | source)
XLA Modules:
  0.0 175.2 jit_solution(10157869390751436851)
XLA Ops:
  0.6 0.0 copy-start.18
  0.6 0.0 copy-start.19
  0.7 1.7 pack_keys.1
  2.4 0.8 collective-permute-start.1
  3.2 6.0 %collective-permute-done.1 = bf16[384,256]{1,0:T(8,128)(2,1)S(1)} collective-permute-done((bf16[384,256]{1,0:T(8,128)(2,1)}, bf16[384,256]{1,0:T(8,128)(2,1)S(1)}, u32[]{:S(2)}, u32[]{:S(2)}) %collective-permute-start.1) | collective-permute-done | bytes 196640 | tf_op jit(solution)/shard_map/ppermute | solution.py:346
  9.2 1.0 broadcast_select_fusion
  10.2 1.6 collective-permute-start.9
  11.8 3.7 %turn_queries.1.refs_1_ = bf16[4,256,768]{2,1,0:T(8,128)(2,1)} custom-call(bf16[384,1024]{1,0:T(8,128)(2,1)} %queries.1), custom_call_target="tpu_custom_call" | custom-call | tf_op jit(solution)/shard_map/turn_queries/pallas_call | solution.py:132
  15.5 0.1 rev.3
  15.6 0.1 pad.4.rev
  15.7 0.0 copy-start.6
  15.7 0.0 copy-start.11
  15.7 10.4 %mixed_tail.1 = bf16[176,2048]{1,0:T(8,128)(2,1)} custom-call(bf16[384,2048]{1,0:T(8,128)(2,1)} %one.3, bf16[384,2048]{1,0:T(8,128)(2,1)} %two.3, bf16[384,2048]{1,0:T(8,128)(2,1)} %val.3, bf16[3,7,2048]{2,1,0:T(8,128)(2,1)} %taps.3), custom_call_target="tpu_custom_call" | custom-call | tf_op jit(solution)/shard_map/mixed_tail/pallas_call | solution.py:33
  26.2 0.0 collective-permute-start.2
  26.2 2.0 %collective-permute-start.3 = (bf16[384,256]{1,0:T(8,128)(2,1)S(1)}, bf16[384,256]{1,0:T(8,128)(2,1)S(1)}, u32[]{:S(2)}, u32[]{:S(2)}) collective-permute-start(bf16[384,256]{1,0:T(8,128)(2,1)S(1)} %get-tuple-element.19), channel_id=1, source_target_pairs={{0,48},{4,52},{8,56},{12,60},{16,0},{20,4},{24,8},{28,12},{32,16},... | collective-permute-start | bytes 589832 | tf_op jit(solution)/shard_map/ppermute | solution.py:346
  28.2 0.6 collective-permute-start.4
  28.8 1.7 collective-permute-start.10
  30.4 0.0 collective-permute-done.9
  30.4 2.0 %collective-permute-start.11 = (bf16[384,256]{1,0:T(8,128)(2,1)S(1)}, bf16[384,256]{1,0:T(8,128)(2,1)S(1)}, u32[]{:S(2)}, u32[]{:S(2)}) collective-permute-start(bf16[384,256]{1,0:T(8,128)(2,1)S(1)} %get-tuple-element.18), channel_id=1, source_target_pairs={{0,8},{4,12},{8,0},{12,4},{16,24},{20,28},{24,16},{28,20},{32,40},... | collective-permute-start | bytes 589832 | tf_op jit(solution)/shard_map/ppermute | solution.py:346
  32.4 0.0 copy-done.6
  32.4 8.3 %attend.4 = (f32[4,144,768]{2,1,0:T(8,128)S(1)}, f32[4,8,768]{2,1,0:T(8,128)S(1)}) custom-call(s32[32,8]{1,0:T(8,128)S(1)} %copy-done.11, bf16[4,256,768]{2,1,0:T(8,128)(2,1)S(1)} %copy-done.4, bf16[1,384,256]{2,1,0:T(8,128)(2,1)S(1)} %bitcast.10, bf16[1,384,256]{2,1,0:T(8,128)(2,1)S(1)} %bitcast.23), custom_call_target="tpu_custom_call" | custom-call | flops 2415919104 | bytes 4194304 | tf_op jit(solution)/shard_map/attend/pallas_call | solution.py:286
  40.8 0.0 copy-start.10
  40.8 0.0 collective-permute-done.10
  40.8 0.0 copy-done.17
  40.8 2.6 %collective-permute-start = (bf16[176,2048]{1,0:T(8,128)(2,1)S(1)}, bf16[176,2048]{1,0:T(8,128)(2,1)S(1)}, u32[]{:S(2)}, u32[]{:S(2)}) collective-permute-start(bf16[176,2048]{1,0:T(8,128)(2,1)S(1)} %copy-done.17), channel_id=1, source_target_pairs={{0,4},{4,8},{8,12},{12,16},{16,20},{20,24},{24,28},{28,32},{32,36}... | collective-permute-start | bytes 2162696 | tf_op jit(solution)/shard_map/ppermute | solution.py:384
  43.4 0.0 collective-permute-done.11
  43.4 1.0 pad_maximum_fusion.1
  44.4 2.5 %collective-permute-start.12 = (bf16[4,384,256]{2,1,0:T(8,128)(2,1)}, bf16[4,384,256]{2,1,0:T(8,128)(2,1)}, u32[]{:S(2)}, u32[]{:S(2)}) collective-permute-start(bf16[4,384,256]{2,1,0:T(8,128)(2,1)} %pad_maximum_fusion.1), channel_id=1, source_target_pairs={{0,16},{4,20},{8,24},{12,28},{16,32},{20,36},{24,40},{28,44},{32,4... | collective-permute-start | bytes 2359304 | tf_op jit(solution)/shard_map/ppermute | solution.py:346
  46.9 0.0 collective-permute-done.2
  46.9 0.0 collective-permute-start.14
  46.9 0.0 collective-permute-done.3
  46.9 0.0 collective-permute-done.4
  46.9 1.0 pad_maximum_fusion
  47.9 0.8 collective-permute-start.5
  48.8 2.4 %collective-permute-start.7 = (bf16[4,384,256]{2,1,0:T(8,128)(2,1)}, bf16[4,384,256]{2,1,0:T(8,128)(2,1)}, u32[]{:S(2)}, u32[]{:S(2)}) collective-permute-start(bf16[4,384,256]{2,1,0:T(8,128)(2,1)} %pad_maximum_fusion), channel_id=1, source_target_pairs={{0,12},{4,0},{8,4},{12,8},{16,28},{20,16},{24,20},{28,24},{32,44},... | collective-permute-start | bytes 2359304 | tf_op jit(solution)/shard_map/ppermute | solution.py:346
  51.2 0.0 copy-start.2
  51.2 0.0 copy-start.3
  51.2 0.0 copy-start.7
  51.2 14.7 %attend.5 = (f32[4,144,768]{2,1,0:T(8,128)S(1)}, f32[4,8,768]{2,1,0:T(8,128)S(1)}) custom-call(s32[32,20]{1,0:T(8,128)S(1)} %copy-done.10, bf16[4,256,768]{2,1,0:T(8,128)(2,1)S(1)} %copy-done.4, bf16[1,384,256]{2,1,0:T(8,128)(2,1)S(1)} %bitcast.14, bf16[1,384,256]{2,1,0:T(8,128)(2,1)S(1)} %bitcast.16, bf16[1,384,256]{2,1,0:T(8,128)(2,1)S(1)} %bitcast.18, ...), custom_call_target="tpu_custom_call" | custom-call | flops 7247757312 | bytes 4194304 | tf_op jit(solution)/shard_map/attend/pallas_call | solution.py:286
  65.9 0.6 copy-done.15
  66.5 0.0 collective-permute-done.halo
  66.5 21.4 %mixer.1 = (f32[384,2048]{1,0:T(8,128)S(1)}, f32[384,128]{1,0:T(8,128)S(1)}) custom-call(bf16[384,2048]{1,0:T(8,128)(2,1)S(1)} %copy-done, bf16[384,2048]{1,0:T(8,128)(2,1)S(1)} %copy-done.1, bf16[384,2048]{1,0:T(8,128)(2,1)S(1)} %copy-done.2, bf16[176,2048]{1,0:T(8,128)(2,1)S(1)} %collective-permute-done.halo, bf16[3,7,2048]{2,1,0:T(8,128)(2,1)S(1)} %copy-done.7, ...), custom_call_target="tpu_custom_call" | custom-call | tf_op jit(solution)/shard_map/mixer/pallas_call | solution.py:84
  87.9 0.1 reduce_sum.9
  88.1 7.2 %psum.7 = f32[384]{0:T(512)S(1)} all-reduce(f32[384]{0:T(512)S(1)} %reduce_sum.9), channel_id=1, replica_groups=mesh['ctx'=32,'tp'=4] {'tp'}, use_global_device_ids=true, to_apply=%region_1.2 | all-reduce | flops 384 | bytes 3072 | tf_op jit(solution)/shard_map/psum | solution.py:397
  95.3 1.5 multiply_convert_fusion
  96.7 0.0 collective-permute-done.12.refs_4_
  96.7 1.1 slice.18
  97.9 3.3 %collective-permute-start.13 = (bf16[2,384,256]{2,1,0:T(8,128)(2,1)S(1)}, bf16[2,384,256]{2,1,0:T(8,128)(2,1)S(1)}, u32[]{:S(2)}, u32[]{:S(2)}) collective-permute-start(bf16[2,384,256]{2,1,0:T(8,128)(2,1)S(1)} %slice.18), channel_id=1, source_target_pairs={{0,16},{4,20},{8,24},{12,28},{16,32},{20,36},{24,40},{28,44},{32,4... | collective-permute-start | bytes 1179656 | tf_op jit(solution)/shard_map/ppermute | solution.py:346
  101.2 0.0 collective-permute-done.14.refs_5_
  101.2 1.0 slice.19
  102.2 0.1 collective-permute-start.15
  102.3 0.0 collective-permute-done.5.refs_2_
  102.3 1.0 slice.16
  103.3 0.1 collective-permute-start.6
  103.4 0.0 collective-permute-done.7.refs_3_
  103.4 1.0 slice.17
  104.4 5.8 %collective-permute-start.8 = (bf16[2,384,256]{2,1,0:T(8,128)(2,1)S(1)}, bf16[2,384,256]{2,1,0:T(8,128)(2,1)S(1)}, u32[]{:S(2)}, u32[]{:S(2)}) collective-permute-start(bf16[2,384,256]{2,1,0:T(8,128)(2,1)S(1)} %slice.17), channel_id=1, source_target_pairs={{0,12},{4,0},{8,4},{12,8},{16,28},{20,16},{24,20},{28,24},{32,44},... | collective-permute-start | bytes 1179656 | tf_op jit(solution)/shard_map/ppermute | solution.py:346
  110.2 40.2 %attend.6 = (f32[4,144,768]{2,1,0:T(8,128)}, f32[4,8,768]{2,1,0:T(8,128)S(1)}) custom-call(s32[32,50]{1,0:T(8,128)S(1)} %copy-done.9, bf16[4,256,768]{2,1,0:T(8,128)(2,1)S(1)} %copy-done.5, bf16[4,384,256]{2,1,0:T(8,128)(2,1)} %collective-permute-done.5.refs_2_, bf16[4,384,256]{2,1,0:T(8,128)(2,1)} %collective-permute-done.7.refs_3_, ...), custom_call_target="tpu_custom_call" | custom-call | flops 19327352832 | bytes 4194304 | tf_op jit(solution)/shard_map/attend/pallas_call | solution.py:286
  150.5 0.0 collective-permute-done.13.refs_4_
  150.5 0.0 collective-permute-done.15.refs_5_
  150.5 0.0 collective-permute-done.6.refs_2_
  150.5 0.0 collective-permute-done.8.refs_3_
  150.6 1.5 copy-done.14
  152.0 23.0 %attend.7 = bf16[384,1024]{1,0:T(8,128)(2,1)} custom-call(s32[32,26]{1,0:T(8,128)S(1)} %copy-done.8, bf16[4,256,768]{2,1,0:T(8,128)(2,1)S(1)} %copy-done.5, bf16[2,384,256]{2,1,0:T(8,128)(2,1)S(1)} %collective-permute-done.6.refs_2_, bf16[2,384,256]{2,1,0:T(8,128)(2,1)S(1)} %collective-permute-done.8.refs_3_, ...), custom_call_target="tpu_custom_call" | custom-call | flops 9663676416 | bytes 4194304 | tf_op jit(solution)/shard_map/attend/pallas_call | solution.py:286
  (30 shorter events, 0.1 us)
Async XLA Ops:
  0.6 14.9 %copy-start.18 = (bf16[128,128]{1,0:T(8,128)(2,1)S(1)}, bf16[128,128]{1,0:T(8,128)(2,1)}, u32[]{:S(2)}) copy-start(bf16[128,128]{1,0:T(8,128)(2,1)} %param.18) | copy-start | bytes 98308
  0.6 15.0 %copy-start.19 = (bf16[2048]{0:T(1024)(128)(2,1)S(1)}, bf16[2048]{0:T(1024)(128)(2,1)}, u32[]{:S(2)}) copy-start(bf16[2048]{0:T(1024)(128)(2,1)} %param.20) | copy-start | bytes 12292
  2.4 6.9 %collective-permute-start.1 = (bf16[384,256]{1,0:T(8,128)(2,1)}, bf16[384,256]{1,0:T(8,128)(2,1)S(1)}, u32[]{:S(2)}, u32[]{:S(2)}) collective-permute-start(bf16[384,256]{1,0:T(8,128)(2,1)} %pack_keys.1), channel_id=1, source_target_pairs={{0,64},{4,68},{8,72},{12,76},{16,80},{20,84},{24,88},{28,92},{32,9... | collective-permute-start | bytes 589832 | tf_op jit(solution)/shard_map/ppermute | solution.py:346
  10.2 20.2 %collective-permute-start.9 = (bf16[384,256]{1,0:T(8,128)(2,1)S(1)}, bf16[384,256]{1,0:T(8,128)(2,1)S(1)}, u32[]{:S(2)}, u32[]{:S(2)}) collective-permute-start(bf16[384,256]{1,0:T(8,128)(2,1)S(1)} %get-tuple-element.18), channel_id=1, source_target_pairs={{0,4},{4,8},{8,12},{12,0},{16,20},{20,24},{24,28},{28,16},{32,36},... | collective-permute-start | bytes 589832 | tf_op jit(solution)/shard_map/ppermute | solution.py:346
  15.7 16.7 %copy-start.4 = (bf16[4,256,768]{2,1,0:T(8,128)(2,1)S(1)}, bf16[4,256,768]{2,1,0:T(8,128)(2,1)}, u32[]{:S(2)}) copy-start(bf16[4,256,768]{2,1,0:T(8,128)(2,1)} %turn_queries.1.refs_1_) | copy-start | bytes 4718596
  15.7 16.7 %copy-start.6 = (bf16[384,256]{1,0:T(8,128)(2,1)S(1)}, bf16[384,256]{1,0:T(8,128)(2,1)}, u32[]{:S(2)}) copy-start(bf16[384,256]{1,0:T(8,128)(2,1)} %pack_keys.1) | copy-start | bytes 589828
  15.7 16.7 %copy-start.11 = (s32[32,8]{1,0:T(8,128)S(1)}, s32[32,8]{1,0:T(8,128)}, u32[]{:S(2)}) copy-start(s32[32,8]{1,0:T(8,128)} %constant.25.clone.refs_0_) | copy-start | bytes 3076
  26.2 20.8 %collective-permute-start.2 = (bf16[384,256]{1,0:T(8,128)(2,1)S(1)}, bf16[384,256]{1,0:T(8,128)(2,1)S(1)}, u32[]{:S(2)}, u32[]{:S(2)}) collective-permute-start(bf16[384,256]{1,0:T(8,128)(2,1)S(1)} %get-tuple-element.19), channel_id=1, source_target_pairs={{0,16},{4,20},{8,24},{12,28},{16,32},{20,36},{24,40},{28,44},{32,4... | collective-permute-start | bytes 589832 | tf_op jit(solution)/shard_map/ppermute | solution.py:346
  26.2 20.8 %collective-permute-start.3 = (bf16[384,256]{1,0:T(8,128)(2,1)S(1)}, bf16[384,256]{1,0:T(8,128)(2,1)S(1)}, u32[]{:S(2)}, u32[]{:S(2)}) collective-permute-start(bf16[384,256]{1,0:T(8,128)(2,1)S(1)} %get-tuple-element.19), channel_id=1, source_target_pairs={{0,48},{4,52},{8,56},{12,60},{16,0},{20,4},{24,8},{28,12},{32,16},... | collective-permute-start | bytes 589832 | tf_op jit(solution)/shard_map/ppermute | solution.py:346
  28.2 18.7 %collective-permute-start.4 = (bf16[384,256]{1,0:T(8,128)(2,1)S(1)}, bf16[384,256]{1,0:T(8,128)(2,1)S(1)}, u32[]{:S(2)}, u32[]{:S(2)}) collective-permute-start(bf16[384,256]{1,0:T(8,128)(2,1)S(1)} %get-tuple-element.19), channel_id=1, source_target_pairs={{0,32},{4,36},{8,40},{12,44},{16,48},{20,52},{24,56},{28,60},{32,0... | collective-permute-start | bytes 589832 | tf_op jit(solution)/shard_map/ppermute | solution.py:346
  28.8 12.0 %collective-permute-start.10 = (bf16[384,256]{1,0:T(8,128)(2,1)S(1)}, bf16[384,256]{1,0:T(8,128)(2,1)S(1)}, u32[]{:S(2)}, u32[]{:S(2)}) collective-permute-start(bf16[384,256]{1,0:T(8,128)(2,1)S(1)} %get-tuple-element.18), channel_id=1, source_target_pairs={{0,12},{4,0},{8,4},{12,8},{16,28},{20,16},{24,20},{28,24},{32,44},... | collective-permute-start | bytes 589832 | tf_op jit(solution)/shard_map/ppermute | solution.py:346
  30.4 13.0 %collective-permute-start.11 = (bf16[384,256]{1,0:T(8,128)(2,1)S(1)}, bf16[384,256]{1,0:T(8,128)(2,1)S(1)}, u32[]{:S(2)}, u32[]{:S(2)}) collective-permute-start(bf16[384,256]{1,0:T(8,128)(2,1)S(1)} %get-tuple-element.18), channel_id=1, source_target_pairs={{0,8},{4,12},{8,0},{12,4},{16,24},{20,28},{24,16},{28,20},{32,40},... | collective-permute-start | bytes 589832 | tf_op jit(solution)/shard_map/ppermute | solution.py:346
  32.4 8.4 %copy-start.17 = (bf16[176,2048]{1,0:T(8,128)(2,1)S(1)}, bf16[176,2048]{1,0:T(8,128)(2,1)}, u32[]{:S(2)}) copy-start(bf16[176,2048]{1,0:T(8,128)(2,1)} %mixed_tail.1) | copy-start | bytes 2162692
  40.8 10.4 %copy-start.12 = (f32[4,144,768]{2,1,0:T(8,128)}, f32[4,144,768]{2,1,0:T(8,128)S(1)}, u32[]{:S(2)}) copy-start(f32[4,144,768]{2,1,0:T(8,128)S(1)} %get-tuple-element.12.refs_8_) | copy-start | bytes 5308420
  40.8 10.4 %copy-start.10 = (s32[32,20]{1,0:T(8,128)S(1)}, s32[32,20]{1,0:T(8,128)}, u32[]{:S(2)}) copy-start(s32[32,20]{1,0:T(8,128)} %constant.26.clone.refs_0_) | copy-start | bytes 7684
  40.8 25.7 %collective-permute-start = (bf16[176,2048]{1,0:T(8,128)(2,1)S(1)}, bf16[176,2048]{1,0:T(8,128)(2,1)S(1)}, u32[]{:S(2)}, u32[]{:S(2)}) collective-permute-start(bf16[176,2048]{1,0:T(8,128)(2,1)S(1)} %copy-done.17), channel_id=1, source_target_pairs={{0,4},{4,8},{8,12},{12,16},{16,20},{20,24},{24,28},{28,32},{32,36}... | collective-permute-start | bytes 2162696 | tf_op jit(solution)/shard_map/ppermute | solution.py:384
  44.4 52.3 %collective-permute-start.12 = (bf16[4,384,256]{2,1,0:T(8,128)(2,1)}, bf16[4,384,256]{2,1,0:T(8,128)(2,1)}, u32[]{:S(2)}, u32[]{:S(2)}) collective-permute-start(bf16[4,384,256]{2,1,0:T(8,128)(2,1)} %pad_maximum_fusion.1), channel_id=1, source_target_pairs={{0,16},{4,20},{8,24},{12,28},{16,32},{20,36},{24,40},{28,44},{32,4... | collective-permute-start | bytes 2359304 | tf_op jit(solution)/shard_map/ppermute | solution.py:346
  46.9 54.3 %collective-permute-start.14 = (bf16[4,384,256]{2,1,0:T(8,128)(2,1)}, bf16[4,384,256]{2,1,0:T(8,128)(2,1)}, u32[]{:S(2)}, u32[]{:S(2)}) collective-permute-start(bf16[4,384,256]{2,1,0:T(8,128)(2,1)} %pad_maximum_fusion.1), channel_id=1, source_target_pairs={{0,48},{4,52},{8,56},{12,60},{16,0},{20,4},{24,8},{28,12},{32,16},... | collective-permute-start | bytes 2359304 | tf_op jit(solution)/shard_map/ppermute | solution.py:346
  47.9 54.4 %collective-permute-start.5 = (bf16[4,384,256]{2,1,0:T(8,128)(2,1)}, bf16[4,384,256]{2,1,0:T(8,128)(2,1)}, u32[]{:S(2)}, u32[]{:S(2)}) collective-permute-start(bf16[4,384,256]{2,1,0:T(8,128)(2,1)} %pad_maximum_fusion), channel_id=1, source_target_pairs={{0,4},{4,8},{8,12},{12,0},{16,20},{20,24},{24,28},{28,16},{32,36},... | collective-permute-start | bytes 2359304 | tf_op jit(solution)/shard_map/ppermute | solution.py:346
  48.8 54.7 %collective-permute-start.7 = (bf16[4,384,256]{2,1,0:T(8,128)(2,1)}, bf16[4,384,256]{2,1,0:T(8,128)(2,1)}, u32[]{:S(2)}, u32[]{:S(2)}) collective-permute-start(bf16[4,384,256]{2,1,0:T(8,128)(2,1)} %pad_maximum_fusion), channel_id=1, source_target_pairs={{0,12},{4,0},{8,4},{12,8},{16,28},{20,16},{24,20},{28,24},{32,44},... | collective-permute-start | bytes 2359304 | tf_op jit(solution)/shard_map/ppermute | solution.py:346
  51.2 15.3 %copy-start = (bf16[384,2048]{1,0:T(8,128)(2,1)S(1)}, bf16[384,2048]{1,0:T(8,128)(2,1)}, u32[]{:S(2)}) copy-start(bf16[384,2048]{1,0:T(8,128)(2,1)} %one.3) | copy-start | bytes 4718596
  51.2 15.3 %copy-start.1 = (bf16[384,2048]{1,0:T(8,128)(2,1)S(1)}, bf16[384,2048]{1,0:T(8,128)(2,1)}, u32[]{:S(2)}) copy-start(bf16[384,2048]{1,0:T(8,128)(2,1)} %two.3) | copy-start | bytes 4718596
  51.2 15.3 %copy-start.2 = (bf16[384,2048]{1,0:T(8,128)(2,1)S(1)}, bf16[384,2048]{1,0:T(8,128)(2,1)}, u32[]{:S(2)}) copy-start(bf16[384,2048]{1,0:T(8,128)(2,1)} %val.3) | copy-start | bytes 4718596
  51.2 15.3 %copy-start.3 = (bf16[384,2048]{1,0:T(8,128)(2,1)S(1)}, bf16[384,2048]{1,0:T(8,128)(2,1)}, u32[]{:S(2)}) copy-start(bf16[384,2048]{1,0:T(8,128)(2,1)} %res.1) | copy-start | bytes 4718596
  51.2 15.3 %copy-start.7 = (bf16[3,7,2048]{2,1,0:T(8,128)(2,1)S(1)}, bf16[3,7,2048]{2,1,0:T(8,128)(2,1)}, u32[]{:S(2)}) copy-start(bf16[3,7,2048]{2,1,0:T(8,128)(2,1)} %taps.3) | copy-start | bytes 258052
  65.9 0.6 copy-start.15
  66.5 21.4 %copy-start.13 = (f32[4,144,768]{2,1,0:T(8,128)}, f32[4,144,768]{2,1,0:T(8,128)S(1)}, u32[]{:S(2)}) copy-start(f32[4,144,768]{2,1,0:T(8,128)S(1)} %get-tuple-element.14.refs_6_) | copy-start | bytes 5308420
  96.7 13.5 %copy-start.5 = (bf16[4,256,768]{2,1,0:T(8,128)(2,1)S(1)}, bf16[4,256,768]{2,1,0:T(8,128)(2,1)}, u32[]{:S(2)}) copy-start(bf16[4,256,768]{2,1,0:T(8,128)(2,1)} %turn_queries.1.refs_1_) | copy-start | bytes 4718596
  96.7 13.5 %copy-start.9 = (s32[32,50]{1,0:T(8,128)S(1)}, s32[32,50]{1,0:T(8,128)}, u32[]{:S(2)}) copy-start(s32[32,50]{1,0:T(8,128)} %constant.27.clone.refs_0_) | copy-start | bytes 19204
  96.7 13.5 %copy-start.16 = (f32[4,8,768]{2,1,0:T(8,128)S(1)}, f32[4,8,768]{2,1,0:T(8,128)}, u32[]{:S(2)}) copy-start(f32[4,8,768]{2,1,0:T(8,128)} %copy-done.15) | copy-start | bytes 294916
  97.9 52.6 %collective-permute-start.13 = (bf16[2,384,256]{2,1,0:T(8,128)(2,1)S(1)}, bf16[2,384,256]{2,1,0:T(8,128)(2,1)S(1)}, u32[]{:S(2)}, u32[]{:S(2)}) collective-permute-start(bf16[2,384,256]{2,1,0:T(8,128)(2,1)S(1)} %slice.18), channel_id=1, source_target_pairs={{0,16},{4,20},{8,24},{12,28},{16,32},{20,36},{24,40},{28,44},{32,4... | collective-permute-start | bytes 1179656 | tf_op jit(solution)/shard_map/ppermute | solution.py:346
  102.2 48.3 %collective-permute-start.15 = (bf16[2,384,256]{2,1,0:T(8,128)(2,1)S(1)}, bf16[2,384,256]{2,1,0:T(8,128)(2,1)S(1)}, u32[]{:S(2)}, u32[]{:S(2)}) collective-permute-start(bf16[2,384,256]{2,1,0:T(8,128)(2,1)S(1)} %slice.19), channel_id=1, source_target_pairs={{0,48},{4,52},{8,56},{12,60},{16,0},{20,4},{24,8},{28,12},{32,16},... | collective-permute-start | bytes 1179656 | tf_op jit(solution)/shard_map/ppermute | solution.py:346
  103.3 47.2 %collective-permute-start.6 = (bf16[2,384,256]{2,1,0:T(8,128)(2,1)S(1)}, bf16[2,384,256]{2,1,0:T(8,128)(2,1)S(1)}, u32[]{:S(2)}, u32[]{:S(2)}) collective-permute-start(bf16[2,384,256]{2,1,0:T(8,128)(2,1)S(1)} %slice.16), channel_id=1, source_target_pairs={{0,4},{4,8},{8,12},{12,0},{16,20},{20,24},{24,28},{28,16},{32,36},... | collective-permute-start | bytes 1179656 | tf_op jit(solution)/shard_map/ppermute | solution.py:346
  104.4 46.1 %collective-permute-start.8 = (bf16[2,384,256]{2,1,0:T(8,128)(2,1)S(1)}, bf16[2,384,256]{2,1,0:T(8,128)(2,1)S(1)}, u32[]{:S(2)}, u32[]{:S(2)}) collective-permute-start(bf16[2,384,256]{2,1,0:T(8,128)(2,1)S(1)} %slice.17), channel_id=1, source_target_pairs={{0,12},{4,0},{8,4},{12,8},{16,28},{20,16},{24,20},{28,24},{32,44},... | collective-permute-start | bytes 1179656 | tf_op jit(solution)/shard_map/ppermute | solution.py:346
  110.2 40.3 %copy-start.8 = (s32[32,26]{1,0:T(8,128)S(1)}, s32[32,26]{1,0:T(8,128)}, u32[]{:S(2)}) copy-start(s32[32,26]{1,0:T(8,128)} %constant.28.clone.refs_0_) | copy-start | bytes 9988
  150.6 1.5 copy-start.14
